TPU v7x, 32 devices: a whole 2x2x4 slice. The times are simulated.
32 devices in a mesh: groups: 2 (over y), tp: 4 (over x, core), rep: 4 (over z).
Axes of the slice: x: 2, y: 2, z: 4, core: 2. Of those that a mesh axis runs over, the one named last changes fastest.
Arguments:
- hidden: bfloat16 [768, 8192], P(('groups', 'rep')), parts along dimension 0, may hold values from -6 to 6
- learner_weights: bfloat16 [2, 16384, 4096], P(None, ('groups', 'tp', 'rep')), parts along dimension 1, may hold values from -0.09375 to 0.09375
- slot_cols: int32 [2, 128, 4, 8], P(None, 'groups'), parts along dimension 1, may hold values from 0 to 8, as said below
- cache_keys: bfloat16 [768, 16, 128, 128], P(('groups', 'rep'), 'tp'), parts along dimension 0, may hold values from -700 to 700
- cache_values: bfloat16 [768, 16, 128, 128], P(('groups', 'rep'), 'tp'), parts along dimension 0, may hold values from -6 to 6
- new_keys: bfloat16 [4, 768, 16, 128], P(None, ('groups', 'rep'), 'tp'), parts along dimension 1, may hold values from -6 to 6
- new_values: bfloat16 [4, 768, 16, 128], P(None, ('groups', 'rep'), 'tp'), parts along dimension 1, may hold values from -6 to 6
- cache_len: int32 [768], P(('groups', 'rep')), parts along dimension 0, may hold values from 32 to 128, as said below
Outputs:
- state_out: bfloat16 [768, 8192], P(('groups', 'rep')), parts along dimension 0
There are 2 independent parts, one for each index of `groups`. A program takes and returns all parts, laid end to end along the dimension named above; each array names one. Nothing has to cross between parts.
Inputs may be any that keep to these rules, and one draw needn't show every extreme that they name: `slot_cols`: for each projection, block row i and tp index o, the first entries are the kept local blocks u in rising order and the remaining entries equal 8; how many blocks an index of tp keeps differs widely from index to index. `cache_len`: some row holds exactly 128 cached positions.
All inputs are finite; a program needn't handle non-finite values.
Results may differ from a plain program's by a relative error of at most 0.025.
Values may be sent and summed in bfloat16 or wider, within the bound.
A program may use at most 256 MiB of HBM per device.

v0:
```python
import jax
import jax.numpy as jnp
from jax import lax
from jax.sharding import PartitionSpec as P

HD = 128
STEPS = 4


def normalize(state):
    return (state * lax.rsqrt(jnp.mean(state * state, axis=-1, keepdims=True) + 1e-05)).astype(
        jnp.bfloat16
    )


def on_device(
    hidden, learner_weights, slot_cols, cache_keys, cache_values, new_keys, new_values, cache_len
):
    tp_count = lax.axis_size("tp")
    rep_count = lax.axis_size("rep")
    rows_dev = hidden.shape[0]
    width = hidden.shape[1]
    row_count = learner_weights.shape[1]
    local_width = slot_cols.shape[3]
    owner_index = lax.axis_index("tp")
    replica_index = lax.axis_index("rep")
    learner_index = owner_index * rep_count + replica_index
    block_count = max(1, row_count // 128)
    first_block = learner_index * row_count // 128
    slot_ids = jnp.arange(local_width, dtype=jnp.int32)
    own_maps = lax.dynamic_slice_in_dim(slot_cols, first_block, block_count, 1)
    row_maps = jnp.repeat(own_maps, row_count // block_count, axis=1)
    pick_table = (row_maps[..., None] == slot_ids).astype(jnp.bfloat16)
    source = learner_weights.reshape(2, row_count, tp_count, local_width, 128)
    send = jnp.einsum(
        "mxosu,mxouk->mosxk", pick_table, source, preferred_element_type=jnp.float32
    ).astype(jnp.bfloat16)
    own_cols = lax.dynamic_slice_in_dim(slot_cols, owner_index, 1, 2).reshape(
        2, slot_cols.shape[1], local_width
    )
    rows_target = jnp.repeat(own_cols, 128, axis=1).reshape(
        2, tp_count, rep_count, row_count, local_width
    )
    place_table = (rows_target[..., None] == slot_ids).astype(jnp.bfloat16)
    arrived = lax.all_to_all(send, "tp", split_axis=1, concat_axis=1, tiled=True)
    copies = lax.all_gather(arrived[:, :, None], "rep", axis=2, tiled=True)
    dense_pair = jnp.einsum(
        "mtrsxk,mtrxsu->mtrxuk", copies, place_table, preferred_element_type=jnp.float32
    )
    dense_pair = dense_pair.astype(jnp.bfloat16).reshape(2, width, local_width * 128)
    query_weight = dense_pair[0]
    output_weight = dense_pair[1]
    slot_count = cache_keys.shape[1]
    cache_length = cache_keys.shape[2]
    head_count = local_width * 128 // HD
    group_size = head_count // slot_count
    live_mask = jnp.arange(cache_length, dtype=jnp.int32)[None, :] < cache_len[:, None]
    state = hidden.astype(jnp.float32)
    for step_index in range(STEPS):
        queries = (
            jnp.dot(normalize(state), query_weight, preferred_element_type=jnp.float32)
            * HD ** (-0.5)
        ).astype(jnp.bfloat16)
        queries = queries.reshape(rows_dev, slot_count, group_size, HD)
        cached_scores = jnp.einsum(
            "rvgd,rvld->rvgl", queries, cache_keys, preferred_element_type=jnp.float32
        )
        cached_scores = jnp.where(live_mask[:, None, None, :], cached_scores, -jnp.inf)
        fresh_scores = jnp.einsum(
            "rvgd,trvd->rvgt",
            queries,
            new_keys[: step_index + 1],
            preferred_element_type=jnp.float32,
        )
        largest = jnp.maximum(jnp.max(cached_scores, axis=-1), jnp.max(fresh_scores, axis=-1))
        cached_exp = jnp.exp(cached_scores - largest[..., None])
        fresh_exp = jnp.exp(fresh_scores - largest[..., None])
        denom_sum = jnp.sum(cached_exp, axis=-1) + jnp.sum(fresh_exp, axis=-1)
        cached_weights = (cached_exp / denom_sum[..., None]).astype(jnp.bfloat16)
        fresh_weights = (fresh_exp / denom_sum[..., None]).astype(jnp.bfloat16)
        attend_attended = jnp.einsum(
            "rvgl,rvld->rvgd", cached_weights, cache_values, preferred_element_type=jnp.float32
        )
        attend_attended = attend_attended + jnp.einsum(
            "rvgt,trvd->rvgd",
            fresh_weights,
            new_values[: step_index + 1],
            preferred_element_type=jnp.float32,
        )
        attended = attend_attended.astype(jnp.bfloat16).reshape(rows_dev, head_count * HD)
        partial_term = lax.dot_general(
            attended, output_weight, (((1,), (1,)), ((), ())), preferred_element_type=jnp.float32
        )
        rounded = lax.optimization_barrier(partial_term.astype(jnp.bfloat16))
        state = state + lax.psum(rounded.astype(jnp.float32).astype(jnp.bfloat16), "tp").astype(
            jnp.float32
        )
    return state.astype(jnp.bfloat16)


def solution(mesh):
    return jax.shard_map(
        on_device,
        mesh=mesh,
        in_specs=(
            P(("groups", "rep"), None),
            P(None, ("groups", "tp", "rep"), None),
            P(None, "groups", None, None),
            P(("groups", "rep"), "tp", None, None),
            P(("groups", "rep"), "tp", None, None),
            P(None, ("groups", "rep"), "tp", None),
            P(None, ("groups", "rep"), "tp", None),
            P(("groups", "rep")),
        ),
        out_specs=P(("groups", "rep"), None),
        check_vma=False,
    )
```

profile of v0, /device:TPU:9, one launch (start us, length us, event | category | flops | bytes accessed | tf_op | source)
XLA Modules:
  0.0 1133.2 jit_solution(11275128678144834224)
XLA Ops:
  7.5 9.4 copy.57
  17.1 13.3 %convert_bitcast_fusion = bf16[2,4,8,512,128]{4,2,3,1,0:T(8,128)(2,1)} fusion(bf16[2,512,4,8,128]{4,3,2,1,0:T(8,128)(2,1)} %bitcast.97, s32[2,512,4,8]{3,1,2,0:T(8,128)S(1)} %bitcast.98), kind=kOutput, calls=%fused_computation.36 | convolution fusion | flops 71565312 | bytes 16908288 | tf_op jit(solution)/shard_map/mxosu,mxouk->mosxk/dot_general | solution.py:35
  30.4 7.2 copy.44
  37.6 100.2 %all_to_all.5 = bf16[2,4,8,512,128]{4,2,3,0,1:T(8,128)(2,1)} all-to-all(bf16[2,4,8,512,128]{4,2,3,0,1:T(8,128)(2,1)} %copy.44), channel_id=1, replica_groups=mesh['groups'=2,'tp'=4,'rep'=4] {'tp'}, dimensions={1} | all-to-all | bytes 16777216 | tf_op jit(solution)/shard_map/all_to_all | solution.py:45
  137.8 8.9 copy.45
  146.9 1.2 copy-done.2
  149.3 556.7 %all-gather.3.cloned.1.call-done = bf16[2,4,32,512,128]{4,3,2,1,0:T(8,128)(2,1)} async-done(((bf16[2,4,8,512,128]{4,3,2,1,0:T(8,128)(2,1)}), bf16[2,4,32,512,128]{4,3,2,1,0:T(8,128)(2,1)}) %all-gather.3.cloned.1.call-update) | async-done | bytes 33554448 | tf_op jit(solution)/shard_map/all_gather | solution.py:46
  706.1 3.7 broadcast_in_dim.31
  709.8 36.6 %fusion.3 = bf16[2,4,4,512,8,128]{5,4,3,2,1,0:T(8,128)(2,1)} fusion(bf16[2,4,4,8,512,128]{5,4,3,2,1,0:T(8,128)(2,1)} %bitcast.87, s32[2,4,4,512,8]{4,3,2,1,0:T(8,128)} %bitcast.86), kind=kOutput, calls=%fused_computation.4 | convolution fusion | flops 286261248 | bytes 67633152 | tf_op jit(solution)/shard_map/mtrsxk,mtrxsu->mtrxuk/dot_general | solution.py:47
  746.4 17.4 %fusion.120 = (bf16[1,4,4,512,8,128]{5,4,3,2,1,0:T(8,128)(2,1)}, bf16[1,4,4,512,8,128]{5,4,3,2,1,0:T(8,128)(2,1)S(1)}) fusion(bf16[2,4,4,512,8,128]{5,4,3,2,1,0:T(8,128)(2,1)} %fusion.3), kind=kLoop, calls=%fused_computation.135 | loop fusion | bytes 67108864 | tf_op jit(solution)/shard_map/slice | solution.py:52
  763.8 5.7 copy-done.4
  769.5 3.6 fusion.81
  774.1 1.4 fusion.116
  775.6 9.7 fusion.121
  785.4 1.1 fusion.89
  786.6 6.8 fusion.71
  793.6 12.2 %fusion.31 = bf16[96,8192]{1,0:T(8,128)(2,1)} fusion(bf16[96,1024]{1,0:T(8,128)(2,1)S(1)} %reshape.146, bf16[1024,8,8,128]{3,2,1,0:T(8,128)(2,1)} %bitcast.88), kind=kOutput, calls=%fused_computation.31 | convolution fusion | flops 1611399168 | bytes 18546688 | tf_op jit(solution)/shard_map/dot_general | solution.py:91
  805.8 1.3 copy.47
  807.1 1.2 copy.48
  808.3 41.3 %all-reduce.5.cloned.1.call-done = bf16[96,8192]{1,0:T(8,128)(2,1)} async-done(((bf16[96,8192]{1,0:T(8,128)(2,1)}), bf16[96,8192]{1,0:T(8,128)(2,1)}) %all-reduce.5.cloned.1.call-update) | async-done | bytes 1572880 | tf_op jit(solution)/shard_map/psum | solution.py:95
  849.6 2.1 multiply_reduce_fusion.2
  851.8 9.5 fusion.78
  862.3 9.8 fusion.122
  873.7 1.1 fusion.90
  874.9 6.6 fusion.96
  883.1 12.3 %fusion.34 = bf16[96,8192]{1,0:T(8,128)(2,1)} fusion(bf16[96,1024]{1,0:T(8,128)(2,1)} %reshape.148, bf16[1024,8,8,128]{3,2,1,0:T(8,128)(2,1)} %bitcast.89), kind=kOutput, calls=%fused_computation.32 | convolution fusion | flops 1611399168 | bytes 18546688 | tf_op jit(solution)/shard_map/dot_general | solution.py:91
  895.5 43.0 %all-reduce.7.cloned.1.call-done = bf16[96,8192]{1,0:T(8,128)(2,1)} async-done(((bf16[96,8192]{1,0:T(8,128)(2,1)}), bf16[96,8192]{1,0:T(8,128)(2,1)}) %all-reduce.7.cloned.1.call-update) | async-done | bytes 1572880 | tf_op jit(solution)/shard_map/psum | solution.py:95
  938.5 2.3 multiply_reduce_fusion.1
  940.8 9.7 fusion.75
  951.6 1.7 fusion.125
  953.3 9.7 fusion.124
  963.1 1.1 fusion.93
  964.2 1.1 fusion.92
  965.4 6.5 fusion.97
  971.9 1.7 fusion.73
  974.4 12.3 %fusion.37 = bf16[96,8192]{1,0:T(8,128)(2,1)} fusion(bf16[96,1024]{1,0:T(8,128)(2,1)} %reshape.150, bf16[1024,8,8,128]{3,2,1,0:T(8,128)(2,1)} %bitcast.90), kind=kOutput, calls=%fused_computation.33 | convolution fusion | flops 1611399168 | bytes 18546688 | tf_op jit(solution)/shard_map/dot_general | solution.py:91
  986.7 43.0 %all-reduce.9.cloned.1.call-done = bf16[96,8192]{1,0:T(8,128)(2,1)} async-done(((bf16[96,8192]{1,0:T(8,128)(2,1)}), bf16[96,8192]{1,0:T(8,128)(2,1)}) %all-reduce.9.cloned.1.call-update) | async-done | bytes 1572880 | tf_op jit(solution)/shard_map/psum | solution.py:95
  1029.7 3.0 multiply_reduce_fusion
  1032.8 9.5 fusion.68
  1043.3 1.7 fusion.127
  1045.1 9.7 fusion.126
  1054.9 1.1 fusion.95
  1056.0 1.1 fusion.94
  1057.1 6.5 fusion.98
  1063.6 1.7 fusion.74
  1066.1 12.3 %fusion.40 = bf16[96,8192]{1,0:T(8,128)(2,1)} fusion(bf16[96,1024]{1,0:T(8,128)(2,1)} %reshape.152, bf16[1024,8,8,128]{3,2,1,0:T(8,128)(2,1)} %bitcast.91), kind=kOutput, calls=%fused_computation.34 | convolution fusion | flops 1611399168 | bytes 18546688 | tf_op jit(solution)/shard_map/dot_general | solution.py:91
  1078.5 43.1 %all-reduce.11.cloned.1.call-done = bf16[96,8192]{1,0:T(8,128)(2,1)} async-done(((bf16[96,8192]{1,0:T(8,128)(2,1)}), bf16[96,8192]{1,0:T(8,128)(2,1)}) %all-reduce.11.cloned.1.call-update) | async-done | bytes 1572880 | tf_op jit(solution)/shard_map/psum | solution.py:95
  1121.5 4.7 add_convert_fusion
  (70 shorter events, 12.2 us)
Async XLA Ops:
  6.5 0.8 copy-start
  6.5 699.5 %all-gather.3.cloned.1.call-start = ((), (), s32[]{:S(2)}) async-start(), calls=%async_computation.5 | async-start | bytes 41943040 | tf_op jit(solution)/shard_map/all_gather | solution.py:46
  146.7 1.4 copy-start.2
  146.7 1.8 copy-start.14
  146.7 1.9 copy-start.8
  146.7 2.6 copy-start.9
  146.7 702.9 %all-reduce.5.cloned.1.call-start = ((), (), s32[]{:S(2)}) async-start(), calls=%async_computation.1 | async-start | bytes 3145728 | tf_op jit(solution)/shard_map/psum | solution.py:95
  763.8 5.7 copy-start.4
  805.7 132.7 %all-reduce.7.cloned.1.call-start = ((), (), s32[]{:S(2)}) async-start(), calls=%async_computation.2 | async-start | bytes 3145728 | tf_op jit(solution)/shard_map/psum | solution.py:95
  849.6 2.2 copy-start.3
  862.3 9.8 copy-start.11
  874.9 6.7 copy-start.12
  895.4 134.3 %all-reduce.9.cloned.1.call-start = ((), (), s32[]{:S(2)}) async-start(), calls=%async_computation.3 | async-start | bytes 3145728 | tf_op jit(solution)/shard_map/psum | solution.py:95
  938.5 2.4 copy-start.5
  965.4 6.5 copy-start.13
  986.7 134.8 %all-reduce.11.cloned.1.call-start = ((), (), s32[]{:S(2)}) async-start(), calls=%async_computation.4 | async-start | bytes 3145728 | tf_op jit(solution)/shard_map/psum | solution.py:95
  1029.7 3.1 copy-start.6
  1029.7 3.1 copy-start.7
  1057.1 6.5 copy-start.10
  1078.4 47.8 %copy-start.1 = (s32[2,64,4,8]{1,3,2,0:T(8,128)S(1)}, s32[2,64,4,8]{1,3,2,0:T(8,128)}, u32[]{:S(2)}) copy-start(s32[2,64,4,8]{1,3,2,0:T(8,128)} %param.10) | copy-start | bytes 49156
Sparse Core Ops, SparseCore 0:
  146.9 559.1 all-gather.2
  805.9 43.6 all-reduce.4
  895.5 42.9 all-reduce.6
  986.8 42.8 all-reduce.8
  1078.6 42.9 all-reduce.10
where the time goes:
time: 1140 us; the launch traced here: 1130 us
  waiting for transfers between devices  727 us (64%)
  matrix products  207 us (18%)
  blocking collectives  100 us (9%)
  local copies, waits for them, and re-layouts  64.7 us (6%)
  other arithmetic  20.5 us (2%)
  between operations  14 us (1%)
    all_gather x1, waiting for transfers between devices, on_device(): copies = lax.all_gather(arrived[:, :, None], 'rep', axis=2, tiled=True)  557 us
    psum x4, waiting for transfers between devices, on_device(): lax.psum(rounded.astype(jnp.float32).astype(jnp.bfloat16), 'tp')  170 us
    all_to_all x1, blocking collectives, on_device(): lax.all_to_all(send, 'tp', split_axis=1, concat_axis=1, tiled=True)  100 us
    dot_general x4, matrix products, on_device(): lax.dot_general(attended, output_weight, (((1,), (1,)), ((), ())), prefer...  49 us
    dot_general x4, matrix products, on_device(): jnp.einsum('rvgd,rvld->rvgl', queries, cache_keys, preferred_element_type...  39 us
    dot_general x1, matrix products, on_device(): jnp.einsum('mtrsxk,mtrxsu->mtrxuk', copies, place_table, preferred_elemen...  36.6 us
    dot_general x4, matrix products, on_device(): jnp.dot(normalize(state), query_weight, preferred_element_type=jnp.float32)  32.2 us
    dot_general x4, matrix products, on_device(): jnp.einsum('rvgl,rvld->rvgd', cached_weights, cache_values, preferred_ele...  26.4 us
  transfers between devices with their start and end apart: 5, of which 5 were waited for; matrix products, arithmetic and copies ran while one was open for 0% of the time, Pallas kernels for 0%

commit v1 on v0

v1 whole, which is shorter than its diff:
```python
import functools

import jax
import jax.numpy as jnp
from jax import lax
from jax.experimental import pallas as pl
from jax.experimental.pallas import tpu as pltpu
from jax.sharding import PartitionSpec as P

HD = 128
STEPS = 4
HALVES = 2
PAD = 16
MESH = pl.DeviceIdType.MESH


def kernel(
    dims,
    hid_ref, weights_ref, mask_ref, keys_ref, values_ref, fresh_k_ref, fresh_v_ref, len_ref,
    out_ref,
    xbuf, wbuf, kbuf, vbuf, qsend, qrecv, qs, atts, abuf, usend, urecv, state,
    load_sem, h_send, h_recv, w_send, w_recv, q_send, q_recv, a_send, a_recv,
    u_send, u_recv, x_send, x_recv, o_send, o_recv,
):
    T, R, C, F, half, slots, group, L, width = dims
    heads_dim = F
    rows = R * half
    me_t = lax.axis_index("tp")
    me_r = lax.axis_index("rep")

    def tp_of(d):
        return lax.rem(me_t + d, T)

    def rep_of(d):
        return lax.rem(me_r + d, R)

    loads = [
        pltpu.make_async_copy(keys_ref, kbuf.at[:, :, pl.ds(0, L), :], load_sem.at[0]),
        pltpu.make_async_copy(values_ref, vbuf.at[:, :, pl.ds(0, L), :], load_sem.at[1]),
        pltpu.make_async_copy(fresh_k_ref, kbuf.at[:, :, pl.ds(L, PAD), :], load_sem.at[2]),
        pltpu.make_async_copy(fresh_v_ref, vbuf.at[:, :, pl.ds(L, PAD), :], load_sem.at[3]),
    ]
    columns_own = pl.ds(pl.multiple_of(me_t * F, F), F)
    own_w = [
        pltpu.make_async_copy(weights_ref.at[m, :, columns_own], wbuf.at[m, me_t], load_sem.at[4 + m])
        for m in range(2)
    ]
    own_h = pltpu.make_async_copy(hid_ref.at[me_r], xbuf.at[:, :, me_r], load_sem.at[6])

    barrier = pltpu.get_barrier_semaphore()
    for d in range(1, T):
        pl.semaphore_signal(barrier, inc=1, device_id={"tp": tp_of(d)}, device_id_type=MESH)
    for d in range(1, R):
        pl.semaphore_signal(barrier, inc=1, device_id={"rep": rep_of(d)}, device_id_type=MESH)
    pl.semaphore_wait(barrier, T - 1 + R - 1)

    def w_copy(m, d):
        to = tp_of(d)
        return pltpu.make_async_remote_copy(
            src_ref=weights_ref.at[m, :, pl.ds(pl.multiple_of(to * F, F), F)],
            dst_ref=wbuf.at[m, me_t],
            send_sem=w_send.at[m, d], recv_sem=w_recv.at[m, d],
            device_id={"tp": to}, device_id_type=MESH,
        )

    def h_copy(d):
        to = rep_of(d)
        return pltpu.make_async_remote_copy(
            src_ref=hid_ref.at[to], dst_ref=xbuf.at[:, :, me_r],
            send_sem=h_send.at[d], recv_sem=h_recv.at[d],
            device_id={"rep": to}, device_id_type=MESH,
        )

    def q_copy(b, d):
        to = rep_of(d)
        return pltpu.make_async_remote_copy(
            src_ref=qsend.at[b, to], dst_ref=qrecv.at[b, me_r],
            send_sem=q_send.at[b, d], recv_sem=q_recv.at[b, d],
            device_id={"rep": to}, device_id_type=MESH,
        )

    def a_copy(b, d):
        return pltpu.make_async_remote_copy(
            src_ref=abuf.at[b, me_r], dst_ref=abuf.at[b, me_r],
            send_sem=a_send.at[b, d], recv_sem=a_recv.at[b, d],
            device_id={"rep": rep_of(d)}, device_id_type=MESH,
        )

    def u_copy(b, d):
        to = tp_of(d)
        return pltpu.make_async_remote_copy(
            src_ref=usend.at[b, to], dst_ref=urecv.at[b, me_t],
            send_sem=u_send.at[b, d], recv_sem=u_recv.at[b, d],
            device_id={"tp": to}, device_id_type=MESH,
        )

    def x_copy(b, d):
        return pltpu.make_async_remote_copy(
            src_ref=xbuf.at[b, me_t], dst_ref=xbuf.at[b, me_t],
            send_sem=x_send.at[b, d], recv_sem=x_recv.at[b, d],
            device_id={"tp": tp_of(d)}, device_id_type=MESH,
        )

    def o_copy(b, d):
        to = rep_of(d)
        return pltpu.make_async_remote_copy(
            src_ref=xbuf.at[b, :, to], dst_ref=out_ref.at[me_r, b],
            send_sem=o_send.at[b, d], recv_sem=o_recv.at[b, d],
            device_id={"rep": to}, device_id_type=MESH,
        )

    def mask_weights(m):
        own_w[m].wait()
        for d in range(1, T):
            w_copy(m, d).wait_recv()
        blocks = mask_ref.shape[2]
        side = C // blocks

        @pl.loop(0, T * blocks)
        def _(i):
            t, c = i // blocks, i % blocks
            at = pl.ds(pl.multiple_of(c * side, side), side)
            kept = mask_ref[m, t, c] > 0.5
            block = wbuf[m, t, at, :]
            wbuf[m, t, at, :] = jnp.where(kept, block.astype(jnp.float32), 0.0).astype(jnp.bfloat16)

    tile = min(256, F)

    def q_phase(b):
        @pl.loop(0, F // tile)
        def _(n):
            at = pl.ds(pl.multiple_of(n * tile, tile), tile)
            acc = jnp.zeros((rows, tile), jnp.float32)
            for t in range(T):
                acc += jnp.dot(
                    xbuf[b, t].reshape(rows, C), wbuf[0, t, :, at], preferred_element_type=jnp.float32
                )
            qsend[b, :, :, at] = acc.astype(jnp.bfloat16).reshape(R, half, tile)

        squares = jnp.zeros((rows, 1), jnp.float32)
        for t in range(T):
            x = xbuf[b, t].reshape(rows, C).astype(jnp.float32)
            squares += jnp.sum(x * x, axis=-1, keepdims=True)
        high = squares.astype(jnp.bfloat16).astype(jnp.float32)
        low = squares - high
        lane = lax.broadcasted_iota(jnp.int32, (rows, 128), 1)
        pair = jnp.where(lane < 64, high, low).astype(jnp.bfloat16)
        qsend[b, :, :, pl.ds(F, 128)] = pair.reshape(R, half, 128)
        for d in range(1, R):
            q_copy(b, d).start()
        qrecv[b, me_r] = qsend[b, me_r]

    def a_phase(b, step):
        for d in range(1, R):
            q_copy(b, d).wait_recv()
        squares = jnp.zeros((half, 128), jnp.float32)
        total = jnp.zeros((half, F), jnp.float32)
        for r in range(R):
            squares += qrecv[b, r, :, pl.ds(F, 128)].astype(jnp.float32)
            total += qrecv[b, r, :, pl.ds(0, F)].astype(jnp.float32)
        mean = (squares[:, 0:1] + squares[:, 64:65]) / width
        qs[...] = total * (lax.rsqrt(mean + 1e-05) * HD ** (-0.5))

        @pl.loop(0, half // 8)
        def _(g):
            at = pl.ds(pl.multiple_of(g * 8, 8), 8)
            first = b * half + g * 8
            length = len_ref[pl.ds(pl.multiple_of(first, 8), 8), :]
            length = jnp.concatenate([length] * group, axis=0)
            pos = lax.broadcasted_iota(jnp.int32, (8 * group, L + PAD), 1)
            live = (pos < length) | ((pos >= L) & (pos <= L + step))
            row = lax.rem(lax.broadcasted_iota(jnp.int32, (8 * group, 1), 0), 8)
            for v in range(slots):
                heads = [qs[at, (v * group + k) * HD : (v * group + k + 1) * HD] for k in range(group)]
                query = jnp.concatenate(heads, axis=0).astype(jnp.bfloat16)
                scores = jnp.zeros((8 * group, L + PAD), jnp.float32)
                for i in range(8):
                    one = lax.dot_general(
                        query, kbuf[first + i, v], (((1,), (1,)), ((), ())),
                        preferred_element_type=jnp.float32,
                    )
                    scores = jnp.where(row == i, one, scores)
                scores = jnp.where(live, scores, -jnp.inf)
                top = jnp.max(scores, axis=-1, keepdims=True)
                weights = jnp.exp(scores - top)
                probs = (weights / jnp.sum(weights, axis=-1, keepdims=True)).astype(jnp.bfloat16)
                result = jnp.zeros((8 * group, HD), jnp.float32)
                for i in range(8):
                    one = jnp.dot(probs, vbuf[first + i, v], preferred_element_type=jnp.float32)
                    result = jnp.where(row == i, one, result)
                for k in range(group):
                    atts[at, (v * group + k) * HD : (v * group + k + 1) * HD] = result[k * 8 : (k + 1) * 8]

        abuf[b, me_r] = atts[...].astype(jnp.bfloat16)
        for d in range(1, R):
            a_copy(b, d).start()
        for d in range(1, R):
            q_copy(b, d).wait_send()

    def o_phase(b):
        for d in range(1, R):
            a_copy(b, d).wait_recv()
        for d in range(1, T):
            to = tp_of(d)
            part = lax.dot_general(
                abuf[b].reshape(rows, F), wbuf[1, to], (((1,), (1,)), ((), ())),
                preferred_element_type=jnp.float32,
            )
            usend[b, to] = part.astype(jnp.bfloat16).reshape(R, half, C)
            u_copy(b, d).start()
        part = lax.dot_general(
            abuf[b].reshape(rows, F), wbuf[1, me_t], (((1,), (1,)), ((), ())),
            preferred_element_type=jnp.float32,
        )
        urecv[b, me_t] = part.astype(jnp.bfloat16).reshape(R, half, C)
        for d in range(1, R):
            a_copy(b, d).wait_send()

    def s_phase(b):
        for d in range(1, T):
            u_copy(b, d).wait_recv()
        total = state[b]
        for t in range(T):
            total += urecv[b, t].astype(jnp.float32)
        state[b] = total
        xbuf[b, me_t] = total.astype(jnp.bfloat16)
        for d in range(1, T):
            x_copy(b, d).start()
        for d in range(1, T):
            u_copy(b, d).wait_send()

    def x_wait(b):
        for d in range(1, T):
            x_copy(b, d).wait_recv()
        for d in range(1, T):
            x_copy(b, d).wait_send()

    for d in range(1, T):
        w_copy(0, d).start()
    for d in range(1, R):
        h_copy(d).start()
    own_h.start()
    own_w[0].start()
    for d in range(1, T):
        w_copy(1, d).start()
    own_w[1].start()
    for load in loads:
        load.start()
    own_h.wait()
    for d in range(1, R):
        h_copy(d).wait_recv()
    for b in range(HALVES):
        state[b] = xbuf[b, me_t].astype(jnp.float32)
    mask_weights(0)
    q_phase(0)
    for load in loads:
        load.wait()

    def body(step, carry):
        a_phase(0, step)

        @pl.when(step > 0)
        def _():
            x_wait(1)

        q_phase(1)

        @pl.when(step == 0)
        def _():
            mask_weights(1)

        o_phase(0)
        a_phase(1, step)
        s_phase(0)
        o_phase(1)

        @pl.when(step < STEPS - 1)
        def _():
            x_wait(0)
            q_phase(0)

        s_phase(1)
        return carry

    lax.fori_loop(0, STEPS, body, 0)

    own_o = []
    for b in range(HALVES):
        x_wait(b)
        for d in range(1, R):
            o_copy(b, d).start()
        copy = pltpu.make_async_copy(xbuf.at[b, :, me_r], out_ref.at[me_r, b], load_sem.at[7 + b])
        copy.start()
        own_o.append(copy)
    for b in range(HALVES):
        own_o[b].wait()
        for d in range(1, R):
            o_copy(b, d).wait()
    for d in range(1, R):
        h_copy(d).wait_send()
    for m in range(2):
        for d in range(1, T):
            w_copy(m, d).wait_send()


def on_device(
    hidden, learner_weights, slot_cols, cache_keys, cache_values, new_keys, new_values, cache_len
):
    T = lax.axis_size("tp")
    R = lax.axis_size("rep")
    rows_dev, width = hidden.shape
    C = learner_weights.shape[1]
    F = learner_weights.shape[2] // T
    local_width = slot_cols.shape[3]
    slots, L = cache_keys.shape[1], cache_keys.shape[2]
    group = F // HD // slots
    half = rows_dev // HALVES
    me_t = lax.axis_index("tp")
    me_r = lax.axis_index("rep")

    hid = hidden.reshape(HALVES, half, T, R, C).transpose(3, 0, 2, 1, 4)
    blocks = max(1, C // 128)
    firsts = (jnp.arange(T)[:, None] * R + me_r) * C + jnp.arange(blocks)[None, :] * (C // blocks)
    own_cols = lax.dynamic_index_in_dim(slot_cols, me_t, 2, keepdims=False)
    live = jnp.any(own_cols[..., None] == jnp.arange(local_width, dtype=jnp.int32), axis=-2)
    live = jnp.take(live, firsts.reshape(-1) // 128, axis=1).astype(jnp.float32)
    mask = jnp.repeat(live, 128, axis=-1).reshape(2, T, blocks, 1, F)
    fresh_k = jnp.pad(new_keys.transpose(1, 2, 0, 3), ((0, 0), (0, 0), (0, PAD - STEPS), (0, 0)))
    fresh_v = jnp.pad(new_values.transpose(1, 2, 0, 3), ((0, 0), (0, 0), (0, PAD - STEPS), (0, 0)))
    dims = (T, R, C, F, half, slots, group, L, width)
    bf16, f32 = jnp.bfloat16, jnp.float32
    any_spec = pl.BlockSpec(memory_space=pl.ANY)
    vmem = pl.BlockSpec(memory_space=pltpu.VMEM)
    dma = pltpu.SemaphoreType.DMA
    flops = 2 * rows_dev * R * T * C * F * 2 * STEPS
    out = pl.pallas_call(
        functools.partial(kernel, dims),
        out_shape=jax.ShapeDtypeStruct((R, HALVES, T, half, C), bf16),
        in_specs=[any_spec, any_spec, vmem, any_spec, any_spec, any_spec, any_spec, vmem],
        out_specs=any_spec,
        scratch_shapes=[
            pltpu.VMEM((HALVES, T, R, half, C), bf16),
            pltpu.VMEM((2, T, C, F), bf16),
            pltpu.VMEM((rows_dev, slots, L + PAD, HD), bf16),
            pltpu.VMEM((rows_dev, slots, L + PAD, HD), bf16),
            pltpu.VMEM((HALVES, R, half, F + 128), bf16),
            pltpu.VMEM((HALVES, R, half, F + 128), bf16),
            pltpu.VMEM((half, F), f32),
            pltpu.VMEM((half, F), f32),
            pltpu.VMEM((HALVES, R, half, F), bf16),
            pltpu.VMEM((HALVES, T, R, half, C), bf16),
            pltpu.VMEM((HALVES, T, R, half, C), bf16),
            pltpu.VMEM((HALVES, R, half, C), f32),
            dma((9,)),
            dma((R,)), dma((R,)),
            dma((2, T)), dma((2, T)),
            dma((HALVES, R)), dma((HALVES, R)),
            dma((HALVES, R)), dma((HALVES, R)),
            dma((HALVES, T)), dma((HALVES, T)),
            dma((HALVES, T)), dma((HALVES, T)),
            dma((HALVES, R)), dma((HALVES, R)),
        ],
        compiler_params=pltpu.CompilerParams(
            collective_id=0, has_side_effects=True, vmem_limit_bytes=60 * 1024 * 1024
        ),
        cost_estimate=pl.CostEstimate(flops=flops, bytes_accessed=48 << 20, transcendentals=0),
    )(hid, learner_weights, mask, cache_keys, cache_values, fresh_k, fresh_v, cache_len[:, None])
    return out.transpose(1, 3, 2, 0, 4).reshape(rows_dev, width)


def solution(mesh):
    return jax.shard_map(
        on_device,
        mesh=mesh,
        in_specs=(
            P(("groups", "rep"), None),
            P(None, ("groups", "tp", "rep"), None),
            P(None, "groups", None, None),
            P(("groups", "rep"), "tp", None, None),
            P(("groups", "rep"), "tp", None, None),
            P(None, ("groups", "rep"), "tp", None),
            P(None, ("groups", "rep"), "tp", None),
            P(("groups", "rep")),
        ),
        out_specs=P(("groups", "rep"), None),
        check_vma=False,
    )
```

time: 1140 us -> 382 us (0.34)
  waiting for transfers between devices: 727 us -> 0 us
  Pallas kernels: 0 us -> 364 us
  matrix products: 207 us -> 0 us
  blocking collectives: 100 us -> 0 us
  local copies, waits for them, and re-layouts: 64.7 us -> 17.8 us
  other arithmetic: 20.5 us -> 0.21 us
  between operations: 14 us -> 0.08 us
    all_gather x1 -> x0, waiting for transfers between devices: 557 us -> none  [on_device(): copies = lax.all_gather(arrived[:, :, None], 'rep', axis=2, tiled=True)]
    pallas_call x0 -> x1, Pallas kernels: none -> 364 us  [on_device(): pl.pallas_call(functools.partial(kernel, dims), out_shape=jax.ShapeDtypeS...]
    dot_general x25 -> x0, matrix products: 207 us -> none  [the longest x4 49 us: on_device(): lax.dot_general(attended, output_weight, (((1,), (1,)), ((), ())), prefer...]
    psum x4 -> x0, waiting for transfers between devices: 170 us -> none  [on_device(): lax.psum(rounded.astype(jnp.float32).astype(jnp.bfloat16), 'tp')]
    all_to_all x1 -> x0, blocking collectives: 100 us -> none  [on_device(): lax.all_to_all(send, 'tp', split_axis=1, concat_axis=1, tiled=True)]
    slice x1 -> x0, local copies, waits for them, and re-layouts: 17.4 us -> none  [on_device(): output_weight = dense_pair[1]]
    unnamed x33 -> x6, local copies, waits for them, and re-layouts: 19.7 us -> 3.48 us
    reduce_sum x11 -> x0, other arithmetic: 15.1 us -> none  [the longest x4 7.9 us: normalize(): jnp.mean(state * state, axis=-1, keepdims=True) + 1e-05]
  transfers between devices with their start and end apart: 5 -> 0, of which waited for: 5 -> 0; matrix products, arithmetic and copies ran while one was open for 0% -> 0% of each run, Pallas kernels for 0% -> 0%
where the time goes in v1:
time: 382 us
  Pallas kernels  364 us (95%)
  local copies, waits for them, and re-layouts  17.8 us (5%)
    pallas_call x1, Pallas kernels, on_device(): pl.pallas_call(functools.partial(kernel, dims), out_shape=jax.ShapeDtypeS...  364 us

profile of v1, /device:TPU:9, one launch (start us, length us, event | category | flops | bytes accessed | tf_op | source)
XLA Modules:
  0.0 381.6 jit_solution(17530906682275063323)
XLA Ops:
  0.0 0.0 copy-start
  0.0 0.1 broadcast_add_fusion
  0.1 0.1 add.81
  0.2 0.1 add.78
  0.3 0.5 copy-done
  0.8 0.1 copy.20
  0.9 0.6 gather_fusion
  1.5 0.1 fusion.1
  1.6 1.4 copy.24.len_ref
  3.0 0.8 broadcast_in_dim.22
  3.7 1.5 copy.31
  5.2 1.5 copy.30
  6.8 0.0 copy-start.1
  6.8 1.6 pad.8.fresh_v_ref
  8.3 1.6 pad.7.fresh_k_ref
  9.9 0.0 copy-done.1
  9.9 1.2 reshape.106
  11.1 2.0 copy.29
  13.1 363.5 %shard_map.82 = bf16[4,2,4,48,512]{4,3,2,1,0:T(8,128)(2,1)} custom-call(bf16[4,2,4,48,512]{4,3,2,1,0:T(8,128)(2,1)} %bitcast.18, bf16[2,512,4096]{2,1,0:T(8,128)(2,1)} %weights_ref.1, f32[2,4,4,1,1024]{4,3,2,1,0:T(1,128)} %bitcast.22, bf16[96,4,128,128]{3,2,1,0:T(8,128)(2,1)} %keys_ref.1, bf16[96,4,128,128]{3,2,1,0:T(8,128)(2,1)} %values_ref.1, ...), custom_call_target="tpu_custom_call" | custom-call | flops 12884901888 | bytes 50331648 | tf_op jit(solution)/shard_map/pallas_call | solution.py:336
  376.6 2.6 copy.25
  379.3 2.4 reshape.107
  (7 shorter events, 0.1 us)
Async XLA Ops:
  0.0 0.8 copy-start
  6.8 3.1 copy-start.1

commit v2 on v1

--- a/solution.py
+++ b/solution.py
@@ -9,7 +9,7 @@
 
 HD = 128
 STEPS = 4
-HALVES = 2
+CUTS = 3
 PAD = 16
 MESH = pl.DeviceIdType.MESH
 
@@ -22,9 +22,9 @@
     load_sem, h_send, h_recv, w_send, w_recv, q_send, q_recv, a_send, a_recv,
     u_send, u_recv, x_send, x_recv, o_send, o_recv,
 ):
-    T, R, C, F, half, slots, group, L, width = dims
+    T, R, C, F, cut, slots, group, L, width = dims
     heads_dim = F
-    rows = R * half
+    rows = R * cut
     me_t = lax.axis_index("tp")
     me_r = lax.axis_index("rep")
 
@@ -34,12 +34,18 @@
     def rep_of(d):
         return lax.rem(me_r + d, R)
 
-    loads = [
-        pltpu.make_async_copy(keys_ref, kbuf.at[:, :, pl.ds(0, L), :], load_sem.at[0]),
-        pltpu.make_async_copy(values_ref, vbuf.at[:, :, pl.ds(0, L), :], load_sem.at[1]),
-        pltpu.make_async_copy(fresh_k_ref, kbuf.at[:, :, pl.ds(L, PAD), :], load_sem.at[2]),
-        pltpu.make_async_copy(fresh_v_ref, vbuf.at[:, :, pl.ds(L, PAD), :], load_sem.at[3]),
-    ]
+    loads = []
+    for j in range(2):
+        lanes = pl.ds(j * HD, HD)
+        for source, target, at, depth in (
+            (keys_ref, kbuf, 0, L), (values_ref, vbuf, 0, L),
+            (fresh_k_ref, kbuf, L, PAD), (fresh_v_ref, vbuf, L, PAD),
+        ):
+            loads.append(
+                pltpu.make_async_copy(
+                    source.at[:, j], target.at[:, :, pl.ds(at, depth), lanes], load_sem.at[9 + len(loads)]
+                )
+            )
     columns_own = pl.ds(pl.multiple_of(me_t * F, F), F)
     own_w = [
         pltpu.make_async_copy(weights_ref.at[m, :, columns_own], wbuf.at[m, me_t], load_sem.at[4 + m])
@@ -110,9 +116,6 @@
         )
 
     def mask_weights(m):
-        own_w[m].wait()
-        for d in range(1, T):
-            w_copy(m, d).wait_recv()
         blocks = mask_ref.shape[2]
         side = C // blocks
 
@@ -135,7 +138,7 @@
                 acc += jnp.dot(
                     xbuf[b, t].reshape(rows, C), wbuf[0, t, :, at], preferred_element_type=jnp.float32
                 )
-            qsend[b, :, :, at] = acc.astype(jnp.bfloat16).reshape(R, half, tile)
+            qsend[b, :, :, at] = acc.astype(jnp.bfloat16).reshape(R, cut, tile)
 
         squares = jnp.zeros((rows, 1), jnp.float32)
         for t in range(T):
@@ -145,7 +148,7 @@
         low = squares - high
         lane = lax.broadcasted_iota(jnp.int32, (rows, 128), 1)
         pair = jnp.where(lane < 64, high, low).astype(jnp.bfloat16)
-        qsend[b, :, :, pl.ds(F, 128)] = pair.reshape(R, half, 128)
+        qsend[b, :, :, pl.ds(F, 128)] = pair.reshape(R, cut, 128)
         for d in range(1, R):
             q_copy(b, d).start()
         qrecv[b, me_r] = qsend[b, me_r]
@@ -153,18 +156,19 @@
     def a_phase(b, step):
         for d in range(1, R):
             q_copy(b, d).wait_recv()
-        squares = jnp.zeros((half, 128), jnp.float32)
-        total = jnp.zeros((half, F), jnp.float32)
+        squares = jnp.zeros((cut, 128), jnp.float32)
+        total = jnp.zeros((cut, F), jnp.float32)
         for r in range(R):
             squares += qrecv[b, r, :, pl.ds(F, 128)].astype(jnp.float32)
             total += qrecv[b, r, :, pl.ds(0, F)].astype(jnp.float32)
         mean = (squares[:, 0:1] + squares[:, 64:65]) / width
         qs[...] = total * (lax.rsqrt(mean + 1e-05) * HD ** (-0.5))
 
-        @pl.loop(0, half // 8)
+        @pl.loop(0, cut // 8)
         def _(g):
             at = pl.ds(pl.multiple_of(g * 8, 8), 8)
-            first = b * half + g * 8
+            first = b * cut + g * 8
+            pair_at = b * (cut // 2) + g * 4
             length = len_ref[pl.ds(pl.multiple_of(first, 8), 8), :]
             length = jnp.concatenate([length] * group, axis=0)
             pos = lax.broadcasted_iota(jnp.int32, (8 * group, L + PAD), 1)
@@ -172,22 +176,25 @@
             row = lax.rem(lax.broadcasted_iota(jnp.int32, (8 * group, 1), 0), 8)
             for v in range(slots):
                 heads = [qs[at, (v * group + k) * HD : (v * group + k + 1) * HD] for k in range(group)]
-                query = jnp.concatenate(heads, axis=0).astype(jnp.bfloat16)
+                query = jnp.concatenate(heads, axis=0)
                 scores = jnp.zeros((8 * group, L + PAD), jnp.float32)
-                for i in range(8):
-                    one = lax.dot_general(
-                        query, kbuf[first + i, v], (((1,), (1,)), ((), ())),
+                for i in range(4):
+                    both = jnp.concatenate(
+                        [jnp.where(row == 2 * i + j, query, 0.0) for j in range(2)], axis=1
+                    ).astype(jnp.bfloat16)
+                    scores += lax.dot_general(
+                        both, kbuf[pair_at + i, v], (((1,), (1,)), ((), ())),
                         preferred_element_type=jnp.float32,
                     )
-                    scores = jnp.where(row == i, one, scores)
                 scores = jnp.where(live, scores, -jnp.inf)
                 top = jnp.max(scores, axis=-1, keepdims=True)
                 weights = jnp.exp(scores - top)
                 probs = (weights / jnp.sum(weights, axis=-1, keepdims=True)).astype(jnp.bfloat16)
                 result = jnp.zeros((8 * group, HD), jnp.float32)
-                for i in range(8):
-                    one = jnp.dot(probs, vbuf[first + i, v], preferred_element_type=jnp.float32)
-                    result = jnp.where(row == i, one, result)
+                for i in range(4):
+                    one = jnp.dot(probs, vbuf[pair_at + i, v], preferred_element_type=jnp.float32)
+                    for j in range(2):
+                        result = jnp.where(row == 2 * i + j, one[:, j * HD : (j + 1) * HD], result)
                 for k in range(group):
                     atts[at, (v * group + k) * HD : (v * group + k + 1) * HD] = result[k * 8 : (k + 1) * 8]
 
@@ -206,13 +213,13 @@
                 abuf[b].reshape(rows, F), wbuf[1, to], (((1,), (1,)), ((), ())),
                 preferred_element_type=jnp.float32,
             )
-            usend[b, to] = part.astype(jnp.bfloat16).reshape(R, half, C)
+            usend[b, to] = part.astype(jnp.bfloat16).reshape(R, cut, C)
             u_copy(b, d).start()
         part = lax.dot_general(
             abuf[b].reshape(rows, F), wbuf[1, me_t], (((1,), (1,)), ((), ())),
             preferred_element_type=jnp.float32,
         )
-        urecv[b, me_t] = part.astype(jnp.bfloat16).reshape(R, half, C)
+        urecv[b, me_t] = part.astype(jnp.bfloat16).reshape(R, cut, C)
         for d in range(1, R):
             a_copy(b, d).wait_send()
 
@@ -235,64 +242,97 @@
         for d in range(1, T):
             x_copy(b, d).wait_send()
 
+    own_w[0].start()
     for d in range(1, T):
         w_copy(0, d).start()
     for d in range(1, R):
         h_copy(d).start()
     own_h.start()
-    own_w[0].start()
-    for d in range(1, T):
-        w_copy(1, d).start()
-    own_w[1].start()
     for load in loads:
         load.start()
     own_h.wait()
     for d in range(1, R):
         h_copy(d).wait_recv()
-    for b in range(HALVES):
+    for b in range(CUTS):
         state[b] = xbuf[b, me_t].astype(jnp.float32)
+    own_w[0].wait()
+    for d in range(1, T):
+        w_copy(0, d).wait_recv()
+    own_w[1].start()
+    for d in range(1, T):
+        w_copy(1, d).start()
     mask_weights(0)
-    q_phase(0)
     for load in loads:
         load.wait()
 
     def body(step, carry):
-        a_phase(0, step)
-
-        @pl.when(step > 0)
-        def _():
-            x_wait(1)
-
-        q_phase(1)
+        later = step > 0
+        inside = step < STEPS
+
+        def x_ready(b):
+            @pl.when(later & inside)
+            def _():
+                x_wait(b)
+
+        x_ready(0)
+
+        @pl.when(inside)
+        def _():
+            q_phase(0)
+
+        @pl.when(later)
+        def _():
+            s_phase(1)
+            o_phase(2)
+
+        @pl.when(inside)
+        def _():
+            a_phase(0, step)
+
+        x_ready(1)
+
+        @pl.when(inside)
+        def _():
+            q_phase(1)
+
+        @pl.when(later)
+        def _():
+            s_phase(2)
 
         @pl.when(step == 0)
         def _():
+            own_w[1].wait()
+            for d in range(1, T):
+                w_copy(1, d).wait_recv()
             mask_weights(1)
 
-        o_phase(0)
-        a_phase(1, step)
-        s_phase(0)
-        o_phase(1)
-
-        @pl.when(step < STEPS - 1)
-        def _():
-            x_wait(0)
-            q_phase(0)
-
-        s_phase(1)
+        @pl.when(inside)
+        def _():
+            o_phase(0)
+            a_phase(1, step)
+
+        x_ready(2)
+
+        @pl.when(inside)
+        def _():
+            q_phase(2)
+            s_phase(0)
+            o_phase(1)
+            a_phase(2, step)
+
         return carry
 
-    lax.fori_loop(0, STEPS, body, 0)
+    lax.fori_loop(0, STEPS + 1, body, 0)
 
     own_o = []
-    for b in range(HALVES):
+    for b in range(CUTS):
         x_wait(b)
         for d in range(1, R):
             o_copy(b, d).start()
-        copy = pltpu.make_async_copy(xbuf.at[b, :, me_r], out_ref.at[me_r, b], load_sem.at[7 + b])
+        copy = pltpu.make_async_copy(xbuf.at[b, :, me_r], out_ref.at[me_r, b], load_sem.at[17 + b])
         copy.start()
         own_o.append(copy)
-    for b in range(HALVES):
+    for b in range(CUTS):
         own_o[b].wait()
         for d in range(1, R):
             o_copy(b, d).wait()
@@ -314,11 +354,11 @@
     local_width = slot_cols.shape[3]
     slots, L = cache_keys.shape[1], cache_keys.shape[2]
     group = F // HD // slots
-    half = rows_dev // HALVES
+    cut = rows_dev // CUTS
     me_t = lax.axis_index("tp")
     me_r = lax.axis_index("rep")
 
-    hid = hidden.reshape(HALVES, half, T, R, C).transpose(3, 0, 2, 1, 4)
+    hid = hidden.reshape(CUTS, cut, T, R, C).transpose(3, 0, 2, 1, 4)
     blocks = max(1, C // 128)
     firsts = (jnp.arange(T)[:, None] * R + me_r) * C + jnp.arange(blocks)[None, :] * (C // blocks)
     own_cols = lax.dynamic_index_in_dim(slot_cols, me_t, 2, keepdims=False)
@@ -327,7 +367,7 @@
     mask = jnp.repeat(live, 128, axis=-1).reshape(2, T, blocks, 1, F)
     fresh_k = jnp.pad(new_keys.transpose(1, 2, 0, 3), ((0, 0), (0, 0), (0, PAD - STEPS), (0, 0)))
     fresh_v = jnp.pad(new_values.transpose(1, 2, 0, 3), ((0, 0), (0, 0), (0, PAD - STEPS), (0, 0)))
-    dims = (T, R, C, F, half, slots, group, L, width)
+    dims = (T, R, C, F, cut, slots, group, L, width)
     bf16, f32 = jnp.bfloat16, jnp.float32
     any_spec = pl.BlockSpec(memory_space=pl.ANY)
     vmem = pl.BlockSpec(memory_space=pltpu.VMEM)
@@ -335,36 +375,36 @@
     flops = 2 * rows_dev * R * T * C * F * 2 * STEPS
     out = pl.pallas_call(
         functools.partial(kernel, dims),
-        out_shape=jax.ShapeDtypeStruct((R, HALVES, T, half, C), bf16),
+        out_shape=jax.ShapeDtypeStruct((R, CUTS, T, cut, C), bf16),
         in_specs=[any_spec, any_spec, vmem, any_spec, any_spec, any_spec, any_spec, vmem],
         out_specs=any_spec,
         scratch_shapes=[
-            pltpu.VMEM((HALVES, T, R, half, C), bf16),
+            pltpu.VMEM((CUTS, T, R, cut, C), bf16),
             pltpu.VMEM((2, T, C, F), bf16),
-            pltpu.VMEM((rows_dev, slots, L + PAD, HD), bf16),
-            pltpu.VMEM((rows_dev, slots, L + PAD, HD), bf16),
-            pltpu.VMEM((HALVES, R, half, F + 128), bf16),
-            pltpu.VMEM((HALVES, R, half, F + 128), bf16),
-            pltpu.VMEM((half, F), f32),
-            pltpu.VMEM((half, F), f32),
-            pltpu.VMEM((HALVES, R, half, F), bf16),
-            pltpu.VMEM((HALVES, T, R, half, C), bf16),
-            pltpu.VMEM((HALVES, T, R, half, C), bf16),
-            pltpu.VMEM((HALVES, R, half, C), f32),
-            dma((9,)),
+            pltpu.VMEM((rows_dev // 2, slots, L + PAD, 2 * HD), bf16),
+            pltpu.VMEM((rows_dev // 2, slots, L + PAD, 2 * HD), bf16),
+            pltpu.VMEM((CUTS, R, cut, F + 128), bf16),
+            pltpu.VMEM((CUTS, R, cut, F + 128), bf16),
+            pltpu.VMEM((cut, F), f32),
+            pltpu.VMEM((cut, F), f32),
+            pltpu.VMEM((CUTS, R, cut, F), bf16),
+            pltpu.VMEM((CUTS, T, R, cut, C), bf16),
+            pltpu.VMEM((CUTS, T, R, cut, C), bf16),
+            pltpu.VMEM((CUTS, R, cut, C), f32),
+            dma((9 + 8 + CUTS,)),
             dma((R,)), dma((R,)),
             dma((2, T)), dma((2, T)),
-            dma((HALVES, R)), dma((HALVES, R)),
-            dma((HALVES, R)), dma((HALVES, R)),
-            dma((HALVES, T)), dma((HALVES, T)),
-            dma((HALVES, T)), dma((HALVES, T)),
-            dma((HALVES, R)), dma((HALVES, R)),
+            dma((CUTS, R)), dma((CUTS, R)),
+            dma((CUTS, R)), dma((CUTS, R)),
+            dma((CUTS, T)), dma((CUTS, T)),
+            dma((CUTS, T)), dma((CUTS, T)),
+            dma((CUTS, R)), dma((CUTS, R)),
         ],
         compiler_params=pltpu.CompilerParams(
             collective_id=0, has_side_effects=True, vmem_limit_bytes=60 * 1024 * 1024
         ),
         cost_estimate=pl.CostEstimate(flops=flops, bytes_accessed=48 << 20, transcendentals=0),
-    )(hid, learner_weights, mask, cache_keys, cache_values, fresh_k, fresh_v, cache_len[:, None])
+    )(hid, learner_weights, mask, *(a.reshape(rows_dev // 2, 2, *a.shape[1:]) for a in (cache_keys, cache_values, fresh_k, fresh_v)), cache_len[:, None])
     return out.transpose(1, 3, 2, 0, 4).reshape(rows_dev, width)
 
 

time: 382 us -> 362 us (0.948)
  Pallas kernels: 364 us -> 344 us
    pallas_call x1, Pallas kernels: 364 us -> 344 us  [on_device(): pl.pallas_call(functools.partial(kernel, dims), out_shape=jax.ShapeDtypeS...]
where the time goes in v2:
time: 362 us
  Pallas kernels  344 us (95%)
  local copies, waits for them, and re-layouts  17.8 us (5%)
    pallas_call x1, Pallas kernels, on_device(): pl.pallas_call(functools.partial(kernel, dims), out_shape=jax.ShapeDtypeS...  344 us

profile of v2, /device:TPU:9, one launch (start us, length us, event | category | flops | bytes accessed | tf_op | source)
XLA Modules:
  0.0 362.1 jit_solution(6570069597734908037)
XLA Ops:
  0.0 0.0 copy-start
  0.0 0.1 broadcast_add_fusion
  0.1 0.1 add.81
  0.2 0.1 add.78
  0.3 0.5 copy-done
  0.8 0.1 copy.20
  0.9 0.6 gather_fusion
  1.5 0.1 fusion.1
  1.6 1.4 copy.24.len_ref
  3.0 0.8 broadcast_in_dim.22
  3.7 1.5 copy.26
  5.2 1.5 copy.27
  6.8 0.0 copy-start.1
  6.8 1.6 pad.8.clone
  8.3 1.6 pad.7.clone
  9.9 0.0 copy-done.1
  9.9 1.2 reshape.118
  11.1 2.0 copy.29
  13.1 344.0 %shard_map.82 = bf16[4,3,4,32,512]{4,3,2,1,0:T(8,128)(2,1)} custom-call(bf16[4,3,4,32,512]{4,3,2,1,0:T(8,128)(2,1)} %bitcast.18, bf16[2,512,4096]{2,1,0:T(8,128)(2,1)} %weights_ref.1, f32[2,4,4,1,1024]{4,3,2,1,0:T(1,128)} %bitcast.24, bf16[48,2,4,128,128]{4,3,2,1,0:T(8,128)(2,1)} %bitcast.26, bf16[48,2,4,128,128]{4,3,2,1,0:T(8,128)(2,1)} %bitcast.27, ...), custom_call_target="tpu_custom_call" | custom-call | flops 12884901888 | bytes 50331648 | tf_op jit(solution)/shard_map/pallas_call | solution.py:376
  357.1 2.6 copy.25
  359.7 2.4 reshape.123
  (7 shorter events, 0.1 us)
Async XLA Ops:
  0.0 0.8 copy-start
  6.8 3.1 copy-start.1

commit v3 on v2

--- a/solution.py
+++ b/solution.py
@@ -21,12 +21,15 @@
     xbuf, wbuf, kbuf, vbuf, qsend, qrecv, qs, atts, abuf, usend, urecv, state,
     load_sem, h_send, h_recv, w_send, w_recv, q_send, q_recv, a_send, a_recv,
     u_send, u_recv, x_send, x_recv, o_send, o_recv,
+    hs_send, hs_recv, os_send, os_recv,
 ):
     T, R, C, F, cut, slots, group, L, width = dims
     heads_dim = F
     rows = R * cut
     me_t = lax.axis_index("tp")
     me_r = lax.axis_index("rep")
+    core = lax.rem(me_t, 2)
+    sibling = me_t + 1 - 2 * core
 
     def tp_of(d):
         return lax.rem(me_t + d, T)
@@ -51,7 +54,7 @@
         pltpu.make_async_copy(weights_ref.at[m, :, columns_own], wbuf.at[m, me_t], load_sem.at[4 + m])
         for m in range(2)
     ]
-    own_h = pltpu.make_async_copy(hid_ref.at[me_r], xbuf.at[:, :, me_r], load_sem.at[6])
+    own_h = pltpu.make_async_copy(hid_ref.at[me_r], xbuf.at[:, :, :, me_r], load_sem.at[6])
 
     barrier = pltpu.get_barrier_semaphore()
     for d in range(1, T):
@@ -72,9 +75,17 @@
     def h_copy(d):
         to = rep_of(d)
         return pltpu.make_async_remote_copy(
-            src_ref=hid_ref.at[to], dst_ref=xbuf.at[:, :, me_r],
+            src_ref=hid_ref.at[to, :, :, core], dst_ref=xbuf.at[:, :, core, me_r],
             send_sem=h_send.at[d], recv_sem=h_recv.at[d],
             device_id={"rep": to}, device_id_type=MESH,
+        )
+
+    def h_share(d):
+        at = rep_of(d)
+        return pltpu.make_async_remote_copy(
+            src_ref=xbuf.at[:, :, core, at], dst_ref=xbuf.at[:, :, core, at],
+            send_sem=hs_send.at[d], recv_sem=hs_recv.at[d],
+            device_id={"tp": sibling}, device_id_type=MESH,
         )
 
     def q_copy(b, d):
@@ -102,7 +113,7 @@
 
     def x_copy(b, d):
         return pltpu.make_async_remote_copy(
-            src_ref=xbuf.at[b, me_t], dst_ref=xbuf.at[b, me_t],
+            src_ref=xbuf.at[b, me_t // 2, core], dst_ref=xbuf.at[b, me_t // 2, core],
             send_sem=x_send.at[b, d], recv_sem=x_recv.at[b, d],
             device_id={"tp": tp_of(d)}, device_id_type=MESH,
         )
@@ -110,9 +121,17 @@
     def o_copy(b, d):
         to = rep_of(d)
         return pltpu.make_async_remote_copy(
-            src_ref=xbuf.at[b, :, to], dst_ref=out_ref.at[me_r, b],
+            src_ref=xbuf.at[b, :, core, to], dst_ref=out_ref.at[me_r, b, :, core],
             send_sem=o_send.at[b, d], recv_sem=o_recv.at[b, d],
             device_id={"rep": to}, device_id_type=MESH,
+        )
+
+    def o_share(b, d):
+        at = lax.rem(me_r + R - d, R)
+        return pltpu.make_async_remote_copy(
+            src_ref=out_ref.at[at, b, :, core], dst_ref=out_ref.at[at, b, :, core],
+            send_sem=os_send.at[b, d], recv_sem=os_recv.at[b, d],
+            device_id={"tp": sibling}, device_id_type=MESH,
         )
 
     def mask_weights(m):
@@ -136,13 +155,13 @@
             acc = jnp.zeros((rows, tile), jnp.float32)
             for t in range(T):
                 acc += jnp.dot(
-                    xbuf[b, t].reshape(rows, C), wbuf[0, t, :, at], preferred_element_type=jnp.float32
+                    xbuf[b, t // 2, t % 2].reshape(rows, C), wbuf[0, t, :, at], preferred_element_type=jnp.float32
                 )
             qsend[b, :, :, at] = acc.astype(jnp.bfloat16).reshape(R, cut, tile)
 
         squares = jnp.zeros((rows, 1), jnp.float32)
         for t in range(T):
-            x = xbuf[b, t].reshape(rows, C).astype(jnp.float32)
+            x = xbuf[b, t // 2, t % 2].reshape(rows, C).astype(jnp.float32)
             squares += jnp.sum(x * x, axis=-1, keepdims=True)
         high = squares.astype(jnp.bfloat16).astype(jnp.float32)
         low = squares - high
@@ -174,27 +193,38 @@
             pos = lax.broadcasted_iota(jnp.int32, (8 * group, L + PAD), 1)
             live = (pos < length) | ((pos >= L) & (pos <= L + step))
             row = lax.rem(lax.broadcasted_iota(jnp.int32, (8 * group, 1), 0), 8)
+            parts = []
             for v in range(slots):
                 heads = [qs[at, (v * group + k) * HD : (v * group + k + 1) * HD] for k in range(group)]
                 query = jnp.concatenate(heads, axis=0)
-                scores = jnp.zeros((8 * group, L + PAD), jnp.float32)
+                part = jnp.zeros((8 * group, L + PAD), jnp.float32)
                 for i in range(4):
                     both = jnp.concatenate(
                         [jnp.where(row == 2 * i + j, query, 0.0) for j in range(2)], axis=1
                     ).astype(jnp.bfloat16)
-                    scores += lax.dot_general(
+                    part += lax.dot_general(
                         both, kbuf[pair_at + i, v], (((1,), (1,)), ((), ())),
                         preferred_element_type=jnp.float32,
                     )
-                scores = jnp.where(live, scores, -jnp.inf)
-                top = jnp.max(scores, axis=-1, keepdims=True)
-                weights = jnp.exp(scores - top)
-                probs = (weights / jnp.sum(weights, axis=-1, keepdims=True)).astype(jnp.bfloat16)
+                parts.append(jnp.where(live, part, -jnp.inf))
+            scores = jnp.concatenate(parts, axis=0)
+            weights = jnp.exp(scores - jnp.max(scores, axis=-1, keepdims=True))
+            probs = (weights / jnp.sum(weights, axis=-1, keepdims=True)).astype(jnp.bfloat16)
+            found = [
+                [
+                    jnp.dot(
+                        probs[v * 8 * group : (v + 1) * 8 * group], vbuf[pair_at + i, v],
+                        preferred_element_type=jnp.float32,
+                    )
+                    for i in range(4)
+                ]
+                for v in range(slots)
+            ]
+            for v in range(slots):
                 result = jnp.zeros((8 * group, HD), jnp.float32)
                 for i in range(4):
-                    one = jnp.dot(probs, vbuf[pair_at + i, v], preferred_element_type=jnp.float32)
                     for j in range(2):
-                        result = jnp.where(row == 2 * i + j, one[:, j * HD : (j + 1) * HD], result)
+                        result = jnp.where(row == 2 * i + j, found[v][i][:, j * HD : (j + 1) * HD], result)
                 for k in range(group):
                     atts[at, (v * group + k) * HD : (v * group + k + 1) * HD] = result[k * 8 : (k + 1) * 8]
 
@@ -230,7 +260,7 @@
         for t in range(T):
             total += urecv[b, t].astype(jnp.float32)
         state[b] = total
-        xbuf[b, me_t] = total.astype(jnp.bfloat16)
+        xbuf[b, me_t // 2, core] = total.astype(jnp.bfloat16)
         for d in range(1, T):
             x_copy(b, d).start()
         for d in range(1, T):
@@ -252,9 +282,12 @@
         load.start()
     own_h.wait()
     for d in range(1, R):
-        h_copy(d).wait_recv()
+        h_copy(R - d).wait_recv()
+        h_share(d).start()
+    for d in range(1, R):
+        h_share(d).wait_recv()
     for b in range(CUTS):
-        state[b] = xbuf[b, me_t].astype(jnp.float32)
+        state[b] = xbuf[b, me_t // 2, core].astype(jnp.float32)
     own_w[0].wait()
     for d in range(1, T):
         w_copy(0, d).wait_recv()
@@ -264,6 +297,8 @@
     mask_weights(0)
     for load in loads:
         load.wait()
+    for d in range(1, R):
+        h_share(d).wait_send()
 
     def body(step, carry):
         later = step > 0
@@ -329,13 +364,17 @@
         x_wait(b)
         for d in range(1, R):
             o_copy(b, d).start()
-        copy = pltpu.make_async_copy(xbuf.at[b, :, me_r], out_ref.at[me_r, b], load_sem.at[17 + b])
+        copy = pltpu.make_async_copy(xbuf.at[b, :, :, me_r], out_ref.at[me_r, b], load_sem.at[17 + b])
         copy.start()
         own_o.append(copy)
     for b in range(CUTS):
         own_o[b].wait()
         for d in range(1, R):
             o_copy(b, d).wait()
+            o_share(b, d).start()
+    for b in range(CUTS):
+        for d in range(1, R):
+            o_share(b, d).wait()
     for d in range(1, R):
         h_copy(d).wait_send()
     for m in range(2):
@@ -358,7 +397,7 @@
     me_t = lax.axis_index("tp")
     me_r = lax.axis_index("rep")
 
-    hid = hidden.reshape(CUTS, cut, T, R, C).transpose(3, 0, 2, 1, 4)
+    hid = hidden.reshape(CUTS, cut, T // 2, 2, R, C).transpose(4, 0, 2, 3, 1, 5)
     blocks = max(1, C // 128)
     firsts = (jnp.arange(T)[:, None] * R + me_r) * C + jnp.arange(blocks)[None, :] * (C // blocks)
     own_cols = lax.dynamic_index_in_dim(slot_cols, me_t, 2, keepdims=False)
@@ -375,11 +414,11 @@
     flops = 2 * rows_dev * R * T * C * F * 2 * STEPS
     out = pl.pallas_call(
         functools.partial(kernel, dims),
-        out_shape=jax.ShapeDtypeStruct((R, CUTS, T, cut, C), bf16),
+        out_shape=jax.ShapeDtypeStruct((R, CUTS, T // 2, 2, cut, C), bf16),
         in_specs=[any_spec, any_spec, vmem, any_spec, any_spec, any_spec, any_spec, vmem],
         out_specs=any_spec,
         scratch_shapes=[
-            pltpu.VMEM((CUTS, T, R, cut, C), bf16),
+            pltpu.VMEM((CUTS, T // 2, 2, R, cut, C), bf16),
             pltpu.VMEM((2, T, C, F), bf16),
             pltpu.VMEM((rows_dev // 2, slots, L + PAD, 2 * HD), bf16),
             pltpu.VMEM((rows_dev // 2, slots, L + PAD, 2 * HD), bf16),
@@ -399,13 +438,14 @@
             dma((CUTS, T)), dma((CUTS, T)),
             dma((CUTS, T)), dma((CUTS, T)),
             dma((CUTS, R)), dma((CUTS, R)),
+            dma((R,)), dma((R,)), dma((CUTS, R)), dma((CUTS, R)),
         ],
         compiler_params=pltpu.CompilerParams(
             collective_id=0, has_side_effects=True, vmem_limit_bytes=60 * 1024 * 1024
         ),
         cost_estimate=pl.CostEstimate(flops=flops, bytes_accessed=48 << 20, transcendentals=0),
     )(hid, learner_weights, mask, *(a.reshape(rows_dev // 2, 2, *a.shape[1:]) for a in (cache_keys, cache_values, fresh_k, fresh_v)), cache_len[:, None])
-    return out.transpose(1, 3, 2, 0, 4).reshape(rows_dev, width)
+    return out.transpose(1, 4, 2, 3, 0, 5).reshape(rows_dev, width)
 
 
 def solution(mesh):

time: 362 us -> 299 us (0.83)
  Pallas kernels: 344 us -> 279 us
    pallas_call x1, Pallas kernels: 344 us -> 279 us  [on_device(): pl.pallas_call(functools.partial(kernel, dims), out_shape=jax.ShapeDtypeS...]
where the time goes in v3:
time: 299 us; the launch traced here: 297 us
  Pallas kernels  279 us (93%)
  local copies, waits for them, and re-layouts  17.8 us (6%)
    pallas_call x1, Pallas kernels, on_device(): pl.pallas_call(functools.partial(kernel, dims), out_shape=jax.ShapeDtypeS...  279 us

profile of v3, /device:TPU:9, one launch (start us, length us, event | category | flops | bytes accessed | tf_op | source)
XLA Modules:
  0.0 297.4 jit_solution(17488951513973904338)
XLA Ops:
  0.0 0.0 copy-start
  0.0 0.1 broadcast_add_fusion
  0.1 0.1 add.81
  0.2 0.1 add.78
  0.3 0.5 copy-done
  0.8 0.1 copy.20
  0.9 0.6 gather_fusion
  1.5 0.1 fusion.1
  1.6 1.4 copy.24.len_ref
  3.0 0.8 broadcast_in_dim.22
  3.7 1.5 copy.26
  5.2 1.5 copy.27
  6.8 0.0 copy-start.1
  6.8 1.6 pad.8.clone
  8.3 1.6 pad.7.clone
  9.9 0.0 copy-done.1
  9.9 1.2 reshape.118
  11.1 2.0 copy.29
  13.1 279.3 %shard_map.82 = bf16[4,3,2,2,32,512]{5,4,3,2,1,0:T(8,128)(2,1)} custom-call(bf16[4,3,2,2,32,512]{5,4,3,2,1,0:T(8,128)(2,1)} %bitcast.18, bf16[2,512,4096]{2,1,0:T(8,128)(2,1)} %weights_ref.1, f32[2,4,4,1,1024]{4,3,2,1,0:T(1,128)} %bitcast.24, bf16[48,2,4,128,128]{4,3,2,1,0:T(8,128)(2,1)} %bitcast.26, bf16[48,2,4,128,128]{4,3,2,1,0:T(8,128)(2,1)} %bitcast.27, ...), custom_call_target="tpu_custom_call" | custom-call | flops 12884901888 | bytes 50331648 | tf_op jit(solution)/shard_map/pallas_call | solution.py:415
  292.4 2.6 copy.25
  295.0 2.4 reshape.123
  (7 shorter events, 0.1 us)
Async XLA Ops:
  0.0 0.8 copy-start
  6.8 3.1 %copy-start.1 = (bf16[96,8192]{1,0:T(8,128)(2,1)S(1)}, bf16[96,8192]{1,0:T(8,128)(2,1)}, u32[]{:S(2)}) copy-start(bf16[96,8192]{1,0:T(8,128)(2,1)} %param.8) | copy-start | bytes 4718596
